TPU v7x, 256 devices: a whole 4x4x8 slice. The times are simulated.
256 devices in a mesh: mp: 32 (over x, z_lo, core), dp: 8 (over y, z_hi).
Axes of the slice: x: 4, y: 4, z: 8 (z_hi: 2, z_lo: 4; z = z_hi * 4 + z_lo), core: 2. Of those that a mesh axis runs over, the one named last changes fastest.
Arguments:
- inputs: bfloat16 [2048, 4096], P('dp', 'mp'), may hold values from -6 to 6
- qkv_weight: bfloat16 [4096, 3, 4096], P('dp', None, 'mp'), may hold values from -0.09375 to 0.09375
- out_weight: bfloat16 [4096, 4096], P('mp', 'dp'), may hold values from -0.09375 to 0.09375
- up_weight: bfloat16 [4096, 12288], P('dp', 'mp'), may hold values from -0.09375 to 0.09375
- down_weight: bfloat16 [12288, 4096], P('mp', 'dp'), may hold values from -0.0546875 to 0.0546875
- grad_out: bfloat16 [2048, 4096], P('dp', 'mp'), may hold values from -6 to 6
Outputs:
- layer_out: bfloat16 [2048, 4096], P('dp', 'mp')
- qkv_grad: bfloat16 [4096, 3, 4096], P('dp', None, 'mp')
- out_grad: bfloat16 [4096, 4096], P('mp', 'dp')
- up_grad: bfloat16 [4096, 12288], P('dp', 'mp')
- down_grad: bfloat16 [12288, 4096], P('mp', 'dp')
All inputs are finite; a program needn't handle non-finite values.
Results may differ from a plain program's by a relative error of at most 0.018.
Values may be sent and summed in bfloat16 or wider, within the bound.
A program may use at most 64 MiB of HBM per device.

v0:
```python
import math

import jax
import jax.numpy as jnp
from jax import lax
from jax.sharding import PartitionSpec as P

HEAD_DIM = 128
PATCHES = 256


def normalize(values):
    centre = values - jnp.mean(values, axis=-1, keepdims=True)
    scale_inv = 1.0 / jnp.sqrt(jnp.mean(centre * centre, axis=-1, keepdims=True) + 1e-06)
    return (centre * scale_inv, scale_inv)


def norm_back(normed_hat, scale_inv, upstream):
    first = jnp.mean(upstream, axis=-1, keepdims=True)
    second = jnp.mean(upstream * normed_hat, axis=-1, keepdims=True)
    return scale_inv * (upstream - first - normed_hat * second)


def gelu_value(upper):
    return 0.5 * upper * (1.0 + lax.erf(upper * (1.0 / math.sqrt(2.0))))


def gelu_slope(upper):
    return 0.5 * (1.0 + lax.erf(upper * (1.0 / math.sqrt(2.0)))) + upper * jnp.exp(
        -0.5 * upper * upper
    ) * (1.0 / math.sqrt(2.0 * math.pi))


def shards(inputs, qkv_weight, out_weight, up_weight, down_weight, grad_out):
    whole = lax.all_gather(inputs, "mp", axis=1, tiled=True)
    qkv_full, up_full, out_full, down_full = (
        lax.all_gather(qkv_weight, "dp", axis=0, tiled=True),
        lax.all_gather(up_weight, "dp", axis=0, tiled=True),
        lax.all_gather(out_weight, "dp", axis=1, tiled=True),
        lax.all_gather(down_weight, "dp", axis=1, tiled=True),
    )
    rows, model_width = whole.shape
    images = rows // PATCHES
    width = qkv_full.shape[2]
    local_heads = width // HEAD_DIM
    scale = HEAD_DIM ** (-0.5)
    whole_f = whole.astype(jnp.float32)
    normed = normalize(whole_f)[0].astype(jnp.bfloat16)
    qkv = jnp.dot(
        normed, qkv_full.reshape(model_width, 3 * width), preferred_element_type=jnp.float32
    )
    shape4 = (images, PATCHES, local_heads, HEAD_DIM)
    q_hat, q_inv = normalize(qkv[:, :width].reshape(shape4))
    k_hat, k_inv = normalize(qkv[:, width : 2 * width].reshape(shape4))
    q_normed = q_hat.astype(jnp.bfloat16)
    k_normed = k_hat.astype(jnp.bfloat16)
    v_round = qkv[:, 2 * width :].reshape(shape4).astype(jnp.bfloat16)
    scores = (
        jnp.einsum("iphd,iqhd->ihpq", q_normed, k_normed, preferred_element_type=jnp.float32)
        * scale
    )
    expo = jnp.exp(scores)
    prob = expo / jnp.sum(expo, axis=-1, keepdims=True)
    prob_round = prob.astype(jnp.bfloat16)
    mixed = jnp.einsum("ihpq,iqhd->iphd", prob_round, v_round, preferred_element_type=jnp.float32)
    mixed = mixed.reshape(rows, width).astype(jnp.bfloat16)
    upper = jnp.dot(normed, up_full, preferred_element_type=jnp.float32)
    hidden = gelu_value(upper).astype(jnp.bfloat16)
    attn = jnp.dot(mixed, out_full, preferred_element_type=jnp.float32)
    mlp = jnp.dot(hidden, down_full, preferred_element_type=jnp.float32)
    total = lax.psum_scatter(attn + mlp, "mp", scatter_dimension=1, tiled=True)
    layer_out = (inputs.astype(jnp.float32) + total).astype(jnp.bfloat16)
    upstream = lax.all_gather(grad_out, "mp", axis=1, tiled=True)
    part_down = jnp.dot(hidden.T, upstream, preferred_element_type=jnp.float32)
    part_out = jnp.dot(mixed.T, upstream, preferred_element_type=jnp.float32)
    d_hidden = jnp.dot(upstream, down_full.T, preferred_element_type=jnp.float32)
    d_up = (d_hidden * gelu_slope(upper)).astype(jnp.bfloat16)
    part_up = jnp.dot(normed.T, d_up, preferred_element_type=jnp.float32)
    d_mixed = jnp.dot(upstream, out_full.T, preferred_element_type=jnp.float32).astype(jnp.bfloat16)
    d_mixed = d_mixed.reshape(shape4)
    d_prob = jnp.einsum("iphd,iqhd->ihpq", d_mixed, v_round, preferred_element_type=jnp.float32)
    d_value = jnp.einsum("ihpq,iphd->iqhd", prob_round, d_mixed, preferred_element_type=jnp.float32)
    d_scores = prob * (d_prob - jnp.sum(prob * d_prob, axis=-1, keepdims=True)) * scale
    d_scores = d_scores.astype(jnp.bfloat16)
    d_qn = jnp.einsum("ihpq,iqhd->iphd", d_scores, k_normed, preferred_element_type=jnp.float32)
    d_kn = jnp.einsum("ihpq,iphd->iqhd", d_scores, q_normed, preferred_element_type=jnp.float32)
    d_query = norm_back(q_hat, q_inv, d_qn).reshape(rows, width)
    d_key = norm_back(k_hat, k_inv, d_kn).reshape(rows, width)
    d_qkv = jnp.concatenate([d_query, d_key, d_value.reshape(rows, width)], axis=1).astype(
        jnp.bfloat16
    )
    part_qkv = jnp.dot(normed.T, d_qkv, preferred_element_type=jnp.float32).reshape(
        model_width, 3, width
    )
    qkv_sum, up_sum, out_sum, down_sum = (
        lax.psum_scatter(
            part_qkv.astype(jnp.bfloat16), "dp", scatter_dimension=0, tiled=True
        ).astype(jnp.float32),
        lax.psum_scatter(
            part_up.astype(jnp.bfloat16), "dp", scatter_dimension=0, tiled=True
        ).astype(jnp.float32),
        lax.psum_scatter(
            part_out.astype(jnp.bfloat16), "dp", scatter_dimension=1, tiled=True
        ).astype(jnp.float32),
        lax.psum_scatter(
            part_down.astype(jnp.bfloat16), "dp", scatter_dimension=1, tiled=True
        ).astype(jnp.float32),
    )
    return (
        layer_out,
        qkv_sum.astype(jnp.bfloat16),
        out_sum.astype(jnp.bfloat16),
        up_sum.astype(jnp.bfloat16),
        down_sum.astype(jnp.bfloat16),
    )


def solution(mesh):
    placed = (
        P("dp", "mp"),
        P("dp", None, "mp"),
        P("mp", "dp"),
        P("dp", "mp"),
        P("mp", "dp"),
        P("dp", "mp"),
    )
    return jax.shard_map(
        shards,
        mesh=mesh,
        in_specs=placed,
        out_specs=(P("dp", "mp"), P("dp", None, "mp"), P("mp", "dp"), P("dp", "mp"), P("mp", "dp")),
        check_vma=False,
    )
```

profile of v0, /device:TPU:36, one launch (start us, length us, event | category | flops | bytes accessed | tf_op | source)
XLA Modules:
  0.0 1055.5 jit_solution(1206805528308864980)
XLA Ops:
  7.2 0.7 all-gather.7.cloned.1.call-update
  7.9 1.9 copy.15
  9.9 0.7 all-gather.11.cloned.1.call-update
  12.4 62.7 %all-gather.7.cloned.1.call-done = bf16[256,4096]{1,0:T(8,128)(2,1)} async-done(((bf16[256,128]{1,0:T(8,128)(2,1)}), bf16[256,4096]{1,0:T(8,128)(2,1)}) %all-gather.7.cloned.1.call-update) | async-done | bytes 2097168 | tf_op jit(solution)/shard_map/all_gather | solution.py:35
  75.1 2.1 convert_reduce_fusion
  77.4 0.7 fusion.2
  78.1 93.1 %all-gather.9.cloned.1.call-done = bf16[4096,3,128]{0,2,1:T(8,128)(2,1)} async-done(((bf16[512,3,128]{0,2,1:T(8,128)(2,1)}), bf16[4096,3,128]{0,2,1:T(8,128)(2,1)}) %all-gather.9.cloned.1.call-update) | async-done | bytes 3145744 | tf_op jit(solution)/shard_map/all_gather | solution.py:37
  171.2 3.2 fusion.51
  175.2 0.7 copy-done.5
  176.1 55.0 %all-gather.11.cloned.1.call-done = bf16[128,4096]{1,0:T(8,128)(2,1)} async-done(((bf16[128,512]{1,0:T(8,128)(2,1)}), bf16[128,4096]{1,0:T(8,128)(2,1)}) %all-gather.11.cloned.1.call-update) | async-done | bytes 1048592 | tf_op jit(solution)/shard_map/all_gather | solution.py:39
  231.1 4.0 fusion.56
  235.0 86.0 %all-gather.13.cloned.1.call-done = bf16[4096,384]{1,0:T(8,128)(2,1)} async-done(((bf16[512,384]{1,0:T(8,128)(2,1)}), bf16[4096,384]{1,0:T(8,128)(2,1)}) %all-gather.13.cloned.1.call-update) | async-done | bytes 3145744 | tf_op jit(solution)/shard_map/all_gather | solution.py:38
  321.1 3.2 fusion.49
  324.3 88.3 %all-gather.15.cloned.1.call-done = bf16[384,4096]{1,0:T(8,128)(2,1)} async-done(((bf16[384,512]{1,0:T(8,128)(2,1)}), bf16[384,4096]{1,0:T(8,128)(2,1)}) %all-gather.15.cloned.1.call-update) | async-done | bytes 3145744 | tf_op jit(solution)/shard_map/all_gather | solution.py:40
  412.6 6.4 convolution_add_fusion
  419.1 54.5 %all-gather.17.cloned.1.call-done = bf16[256,4096]{1,0:T(8,128)(2,1)} async-done(((bf16[256,128]{1,0:T(8,128)(2,1)}), bf16[256,4096]{1,0:T(8,128)(2,1)}) %all-gather.17.cloned.1.call-update) | async-done | bytes 2097168 | tf_op jit(solution)/shard_map/all_gather | solution.py:73
  473.5 2.4 convolution_convert_fusion.4
  476.0 1.2 multiply_reduce_fusion
  477.2 1.0 multiply_convert_fusion.1
  478.3 2.3 convolution_convert_fusion.3
  481.9 1.0 fusion.7
  483.4 4.3 convolution_convert_fusion.2
  487.7 4.7 copy.19
  492.6 0.7 copy-done.4
  493.4 7.2 convolution_convert_fusion.1
  500.7 2.7 convolution_convert_fusion
  503.4 100.7 %reduce-scatter.6.cloned.1.call-done = f32[256,128]{1,0:T(8,128)} async-done(((f32[256,4096]{1,0:T(8,128)}), f32[256,128]{1,0:T(8,128)}) %reduce-scatter.6.cloned.1.call-update) | async-done | bytes 131088 | tf_op jit(solution)/shard_map/reduce_scatter | solution.py:71
  604.1 1.5 add_convert_fusion
  605.7 109.1 %reduce-scatter.10.cloned.1.call-done = bf16[128,512]{1,0:T(8,128)(2,1)} async-done(((bf16[128,4096]{1,0:T(8,128)(2,1)}), bf16[128,512]{1,0:T(8,128)(2,1)}) %reduce-scatter.10.cloned.1.call-update) | async-done | bytes 131088 | tf_op jit(solution)/shard_map/reduce_scatter | solution.py:102
  714.8 111.4 %reduce-scatter.8.cloned.1.call-done = bf16[512,3,128]{2,0,1:T(8,128)(2,1)} async-done(((bf16[4096,3,128]{2,0,1:T(8,128)(2,1)}), bf16[512,3,128]{2,0,1:T(8,128)(2,1)}) %reduce-scatter.8.cloned.1.call-update) | async-done | bytes 393232 | tf_op jit(solution)/shard_map/reduce_scatter | solution.py:96
  826.1 110.9 %reduce-scatter.12.cloned.1.call-done = bf16[512,384]{1,0:T(8,128)(2,1)} async-done(((bf16[4096,384]{1,0:T(8,128)(2,1)}), bf16[512,384]{1,0:T(8,128)(2,1)}) %reduce-scatter.12.cloned.1.call-update) | async-done | bytes 393232 | tf_op jit(solution)/shard_map/reduce_scatter | solution.py:99
  937.0 112.0 %reduce-scatter.14.cloned.1.call-done = bf16[384,512]{1,0:T(8,128)(2,1)} async-done(((bf16[384,4096]{1,0:T(8,128)(2,1)}), bf16[384,512]{1,0:T(8,128)(2,1)}) %reduce-scatter.14.cloned.1.call-update) | async-done | bytes 393232 | tf_op jit(solution)/shard_map/reduce_scatter | solution.py:105
  (69 shorter events, 5.0 us)
Async XLA Ops:
  7.2 68.0 %all-gather.7.cloned.1.call-start = ((), (), s32[]{:S(2)}) async-start(), calls=%async_computation.5 | async-start | bytes 2162688 | tf_op jit(solution)/shard_map/all_gather | solution.py:35
  7.9 163.3 %all-gather.9.cloned.1.call-start = ((), (), s32[]{:S(2)}) async-start(), calls=%async_computation.6 | async-start | bytes 3538944 | tf_op jit(solution)/shard_map/all_gather | solution.py:37
  9.9 221.2 %all-gather.11.cloned.1.call-start = ((), (), s32[]{:S(2)}) async-start(), calls=%async_computation.7 | async-start | bytes 1179648 | tf_op jit(solution)/shard_map/all_gather | solution.py:39
  10.6 310.4 %all-gather.13.cloned.1.call-start = ((), (), s32[]{:S(2)}) async-start(), calls=%async_computation.8 | async-start | bytes 3538944 | tf_op jit(solution)/shard_map/all_gather | solution.py:38
  11.2 401.4 %all-gather.15.cloned.1.call-start = ((), (), s32[]{:S(2)}) async-start(), calls=%async_computation.9 | async-start | bytes 3538944 | tf_op jit(solution)/shard_map/all_gather | solution.py:40
  11.8 461.8 %all-gather.17.cloned.1.call-start = ((), (), s32[]{:S(2)}) async-start(), calls=%async_computation.11 | async-start | bytes 2162688 | tf_op jit(solution)/shard_map/all_gather | solution.py:73
  12.4 591.8 %reduce-scatter.6.cloned.1.call-start = ((), (), s32[]{:S(2)}) async-start(), calls=%async_computation.10 | async-start | bytes 4325376 | tf_op jit(solution)/shard_map/reduce_scatter | solution.py:71
  75.1 2.2 copy-start.1
  77.4 243.7 %copy-start.10 = (f32[256]{0:T(256)}, f32[256]{0:T(256)S(1)}, u32[]{:S(2)}) copy-start(f32[256]{0:T(256)S(1)} %broadcast_multiply_fusion.6) | copy-start | bytes 3076
  78.1 243.0 %copy-start.14 = (f32[256]{0:T(256)}, f32[256]{0:T(256)S(1)}, u32[]{:S(2)}) copy-start(f32[256]{0:T(256)S(1)} %add_rsqrt_fusion.2) | copy-start | bytes 3076
  175.1 0.7 copy-start.5
  175.2 59.9 %copy-start.12 = (f32[256]{0:T(256)}, f32[256]{0:T(256)S(1)}, u32[]{:S(2)}) copy-start(f32[256]{0:T(256)S(1)} %get-tuple-element.13) | copy-start | bytes 3076
  176.0 59.0 %copy-start.8 = (bf16[256,128]{0,1:T(8,128)(2,1)}, bf16[256,128]{0,1:T(8,128)(2,1)S(1)}, u32[]{:S(2)}) copy-start(bf16[256,128]{0,1:T(8,128)(2,1)S(1)} %fusion.6) | copy-start | bytes 196612
  324.3 88.3 %copy-start.3 = (f32[256,384]{1,0:T(8,128)}, f32[256,384]{1,0:T(8,128)S(1)}, u32[]{:S(2)}) copy-start(f32[256,384]{1,0:T(8,128)S(1)} %fusion.49) | copy-start | bytes 1179652
  419.0 54.5 %copy-start.2 = (bf16[128,4096]{1,0:T(8,128)(2,1)S(1)}, bf16[128,4096]{1,0:T(8,128)(2,1)}, u32[]{:S(2)}) copy-start(bf16[128,4096]{1,0:T(8,128)(2,1)} %all-gather.11.cloned.1.call-done) | copy-start | bytes 3145732
  419.0 295.8 %reduce-scatter.10.cloned.1.call-start = ((), (), s32[]{:S(2)}) async-start(), calls=%async_computation.13 | async-start | bytes 1179648 | tf_op jit(solution)/shard_map/reduce_scatter | solution.py:102
  473.5 4.7 copy-start
  476.0 2.2 copy-start.9
  478.2 3.6 copy-start.6
  478.3 3.6 copy-start.13
  478.3 5.1 copy-start.11
  478.3 5.1 copy-start.15
  480.6 345.5 %reduce-scatter.8.cloned.1.call-start = ((), (), s32[]{:S(2)}) async-start(), calls=%async_computation.12 | async-start | bytes 3538944 | tf_op jit(solution)/shard_map/reduce_scatter | solution.py:96
  492.4 1.0 copy-start.4
  492.4 444.6 %reduce-scatter.12.cloned.1.call-start = ((), (), s32[]{:S(2)}) async-start(), calls=%async_computation.14 | async-start | bytes 3538944 | tf_op jit(solution)/shard_map/reduce_scatter | solution.py:99
  500.6 103.5 %copy-start.7 = (bf16[256,128]{1,0:T(8,128)(2,1)S(1)}, bf16[256,128]{1,0:T(8,128)(2,1)}, u32[]{:S(2)}) copy-start(bf16[256,128]{1,0:T(8,128)(2,1)} %param.6) | copy-start | bytes 196612
  500.6 548.3 %reduce-scatter.14.cloned.1.call-start = ((), (), s32[]{:S(2)}) async-start(), calls=%async_computation.15 | async-start | bytes 3538944 | tf_op jit(solution)/shard_map/reduce_scatter | solution.py:105
Sparse Core Ops, SparseCore 0:
  9.8 65.3 all-gather.6
  78.2 92.9 all-gather.8
  173.7 57.3 all-gather.10
  233.5 87.4 all-gather.12
  323.4 89.1 all-gather.14
  414.2 59.3 all-gather.16
  476.1 128.0 reduce-scatter.5
  608.7 106.0 reduce-scatter.9
  720.2 105.9 reduce-scatter.7
  830.8 106.2 reduce-scatter.11
  942.4 106.5 reduce-scatter.13
where the time goes:
time: 1060 us
  waiting for transfers between devices  987 us (93%)
  matrix products  39.2 us (4%)
  between operations  14.1 us (1%)
    reduce_scatter x1, waiting for transfers between devices, shards(): lax.psum_scatter(part_down.astype(jnp.bfloat16), 'dp', scatter_dimension=...  112 us
    reduce_scatter x1, waiting for transfers between devices, shards(): lax.psum_scatter(part_qkv.astype(jnp.bfloat16), 'dp', scatter_dimension=0...  111 us
    reduce_scatter x1, waiting for transfers between devices, shards(): lax.psum_scatter(part_up.astype(jnp.bfloat16), 'dp', scatter_dimension=0,...  111 us
    reduce_scatter x1, waiting for transfers between devices, shards(): lax.psum_scatter(part_out.astype(jnp.bfloat16), 'dp', scatter_dimension=1...  109 us
    reduce_scatter x1, waiting for transfers between devices, shards(): total = lax.psum_scatter(attn + mlp, 'mp', scatter_dimension=1, tiled=True)  101 us
    all_gather x1, waiting for transfers between devices, shards(): lax.all_gather(qkv_weight, 'dp', axis=0, tiled=True)  93.1 us
    all_gather x1, waiting for transfers between devices, shards(): lax.all_gather(down_weight, 'dp', axis=1, tiled=True)  88.3 us
    all_gather x1, waiting for transfers between devices, shards(): lax.all_gather(up_weight, 'dp', axis=0, tiled=True)  86 us
  transfers between devices with their start and end apart: 11, of which 11 were waited for; matrix products, arithmetic and copies ran while one was open for 5% of the time, Pallas kernels for 0%

commit v1 on v0

v1 whole, which is shorter than its diff:
```python
import math

import jax
import jax.numpy as jnp
from jax import lax
from jax.experimental import pallas as pl
from jax.experimental.pallas import tpu as pltpu
from jax.sharding import PartitionSpec as P

HEAD = 128
TOK = 256
BF = jnp.bfloat16
F32 = jnp.float32
MESH = pl.DeviceIdType.MESH


def normalize(values):
    centre = values - jnp.mean(values, axis=-1, keepdims=True)
    scale_inv = 1.0 / jnp.sqrt(jnp.mean(centre * centre, axis=-1, keepdims=True) + 1e-06)
    return centre * scale_inv, scale_inv


def norm_back(normed_hat, scale_inv, upstream):
    first = jnp.mean(upstream, axis=-1, keepdims=True)
    second = jnp.mean(upstream * normed_hat, axis=-1, keepdims=True)
    return scale_inv * (upstream - first - normed_hat * second)


def mm(a, b):
    return lax.dot_general(a, b, (((1,), (0,)), ((), ())), preferred_element_type=F32)


def mm_nt(a, b):
    return lax.dot_general(a, b, (((1,), (1,)), ((), ())), preferred_element_type=F32)


def mm_tn(a, b):
    return lax.dot_general(a, b, (((0,), (0,)), ((), ())), preferred_element_type=F32)


def merge_stats(parts, count):
    means = [p[0:1, :] for p in parts]
    mean = sum(means) / len(parts)
    square = sum(p[1:2, :] for p in parts) + count * sum((u - mean) * (u - mean) for u in means)
    return mean, square


def two_rows(first, second, rows):
    place = lax.broadcasted_iota(jnp.int32, (rows, TOK), 0)
    return jnp.where(place == 0, first, jnp.where(place == 1, second, 0.0))


class Copies:
    def __init__(self, send, recv):
        self.send, self.recv, self.used, self.all = send, recv, 0, []

    def take(self, count):
        base = self.used
        self.used += count
        return base

    def make(self, src, dst, device, index):
        return pltpu.make_async_remote_copy(
            src_ref=src,
            dst_ref=dst,
            send_sem=self.send.at[index],
            recv_sem=self.recv.at[index],
            device_id=device,
            device_id_type=MESH,
        )

    def new(self, src, dst, device):
        copy = self.make(src, dst, device, self.take(1))
        self.all.append(copy)
        return copy


N_SEMS = 128


def kernel(
    in_ref, grad_ref, wq_ref, wo_ref, wu_ref, wd_ref,
    lay_ref, gq_ref, go_ref, gu_ref, gd_ref,
    wb, xn, ga, xa, st,
    pg, pq, pu, lg, lq, lu, sg, sq, su, zg, zq, zu,
    am, ah, aq, au,
    lp, lc, s1, lx, s2, lz, s3, fin,
    acc_x, acc_b,
    send, recv, local,
):
    m = lax.axis_index("mp")
    d = lax.axis_index("dp")
    x, zl, c = m // 8, (m // 2) % 4, m % 2
    y, zh = d // 2, d % 2

    def at(x=x, zl=zl, c=c, y=y, zh=zh):
        return {"mp": (x * 4 + zl) * 2 + c, "dp": y * 2 + zh}

    sibling = at(c=1 - c)
    z_peers = [at(zl=(zl + j) % 4) for j in (1, 2, 3)]
    x_peers = [at(x=(x + j) % 4) for j in (1, 2, 3)]
    y_peers = [at(y=(y + k) % 4) for k in (1, 2, 3)]
    far = at(zh=1 - zh)
    swap = at(x=y, zl=2 * zh + zl % 2, y=x, zh=zl // 2)
    stays = jnp.logical_and(x == y, zh == zl // 2)
    moves = jnp.logical_not(stays)

    barrier = pltpu.get_barrier_semaphore()
    near = [sibling, far] + z_peers + x_peers + y_peers
    for device in near:
        pl.semaphore_signal(barrier, inc=1, device_id=device, device_id_type=MESH)

    @pl.when(moves)
    def _():
        pl.semaphore_signal(barrier, inc=1, device_id=swap, device_id_type=MESH)
        pl.semaphore_wait(barrier, len(near) + 1)

    @pl.when(stays)
    def _():
        pl.semaphore_wait(barrier, len(near))

    copies = Copies(send, recv)

    swaps = []

    def swap_start(src, dst):
        remote = copies.make(src, dst, swap, copies.take(1))
        near_copy = pltpu.make_async_copy(src, dst, local.at[len(swaps)])
        swaps.append(remote)

        @pl.when(moves)
        def _():
            remote.start()

        @pl.when(stays)
        def _():
            near_copy.start()

        def wait():
            @pl.when(moves)
            def _():
                remote.wait_recv()

            @pl.when(stays)
            def _():
                near_copy.wait()

        return wait

    def z_start(a):
        block = a.at[c, zl % 2, x * 2 + zl // 2]
        group = [copies.new(block, block, peer) for peer in z_peers]
        for copy in group:
            copy.start()
        return group

    def rows_of(a, who):
        return a.at[c, :, pl.ds(2 * who, 2)]

    def x_start(a):
        block = rows_of(a, x)
        group = [copies.new(block, block, peer) for peer in x_peers]
        for copy in group:
            copy.start()
        return group

    def core_start(a, who):
        block = rows_of(a, who)
        copy = copies.new(block, block, sibling)
        copy.start()
        return copy

    def wait_recv(group):
        for copy in group:
            copy.wait_recv()

    def x_to_core(a, group, cores):
        for j, copy in enumerate(group):
            copy.wait_recv()
            cores.append(core_start(a, (x + 3 - j) % 4))

    def tokens(a, t):
        return jnp.concatenate([a[0, 0, t], a[1, 0, t], a[0, 1, t], a[1, 1, t]], axis=1)

    g_swap = swap_start(grad_ref, ga.at[c, zl % 2, d])

    wb[0:384, :] = wd_ref[...]
    wb[384:512, :] = wo_ref[...]

    block_f = in_ref[...].astype(F32)
    mu = jnp.mean(block_f, axis=-1, keepdims=True)
    centre = block_f - mu
    square = jnp.sum(centre * centre, axis=-1, keepdims=True)
    lane = lax.broadcasted_iota(jnp.int32, (TOK, 128), 1)
    packed = jnp.where(lane == 0, mu, jnp.where(lane == 1, square, 0.0))
    st[0] = packed.T[0:8, :]
    st_core = copies.new(st.at[0], st.at[1], sibling)
    st_core.start()

    g_swap()
    g_z = z_start(ga)

    st_core.wait_recv()
    mean, square = merge_stats([st[0], st[1]], 128.0)
    st[2] = two_rows(mean, square, 8)
    st_z = [copies.new(st.at[2], st.at[3 + j], peer) for j, peer in enumerate(z_peers)]
    for copy in st_z:
        copy.start()

    wait_recv(g_z)
    g_x = x_start(ga)
    g_core = [core_start(ga, x)]

    wait_recv(st_z)
    mean, square = merge_stats([st[2 + j] for j in range(4)], 256.0)
    st[6] = two_rows(mean, square, 8)
    st_x = [copies.new(st.at[6], st.at[7 + j], peer) for j, peer in enumerate(x_peers)]
    for copy in st_x:
        copy.start()
    wait_recv(st_x)
    mean, square = merge_stats([st[6 + j] for j in range(4)], 1024.0)
    inv = 1.0 / jnp.sqrt(square / 4096.0 + 1e-06)
    columns = two_rows(mean, inv, 128).T
    xn[...] = ((block_f - columns[:, 0:1]) * columns[:, 1:2]).astype(BF)
    x_swap = swap_start(xn, xa.at[c, zl % 2, d])

    x_to_core(ga, g_x, g_core)
    x_swap()
    x_z = z_start(xa)
    wait_recv(g_core)

    def product_start(p, land, product):
        base = copies.take(6)

        def turn(i):
            last = i // 6
            k = (i % 3 + 1) * (1 - last)
            own = (i // 3) * (1 - last) + (i - 6) * last
            to_zh = (1 - zh) * (1 - own) + zh * own
            return k, own, ((y + k) % 4) * 2 + to_zh

        def step(i, carry):
            k, own, t = turn(i)
            p[t] = product(t).astype(BF)

            @pl.when(i < 6)
            def _():
                copies.make(
                    p.at[t], land.at[own, k - 1], at(y=(y + k) % 4), base + i
                ).start()

            return carry

        lax.fori_loop(0, 8, step, 0)
        group = []
        for i in range(6):
            k, own = i % 3 + 1, i // 3
            to_zh = zh if own else 1 - zh
            t = ((y + k) % 4) * 2 + to_zh
            group.append(copies.make(p.at[t], land.at[own, k - 1], y_peers[k - 1], base + i))
        copies.all.extend(group)
        return group

    g_y = product_start(pg, lg, lambda t: mm_nt(tokens(ga, t), wb[...]))

    wait_recv(x_z)
    x_x = x_start(xa)
    x_core = [core_start(xa, x)]
    x_to_core(xa, x_x, x_core)
    wait_recv(x_core)
    q_y = product_start(pq, lq, lambda t: mm(tokens(xa, t), wq_ref[...]))
    u_y = product_start(pu, lu, lambda t: mm(tokens(xa, t), wu_ref[...]))

    mine = d
    theirs = y * 2 + 1 - zh

    def total(p, land, own, t):
        out = p[t].astype(F32)
        for k in range(3):
            out = out + land[own, k].astype(F32)
        return out

    def far_start(group, p, land, s, z):
        wait_recv(group[:3])
        s[...] = total(p, land, 0, theirs).astype(BF)
        copy = copies.new(s, z, far)
        copy.start()
        return copy

    def finish(group, copy, p, land, z):
        wait_recv(group[3:])
        copy.wait_recv()
        return total(p, land, 1, mine) + z[...].astype(F32)

    g_far = far_start(g_y, pg, lg, sg, zg)
    q_far = far_start(q_y, pq, lq, sq, zq)
    d_both = finish(g_y, g_far, pg, lg, zg)
    sg_hidden = d_both[:, :384]
    d_mixed = d_both[:, 384:].astype(BF)

    qkv = finish(q_y, q_far, pq, lq, zq)
    u_far = far_start(u_y, pu, lu, su, zu)

    scale = HEAD ** (-0.5)
    q_hat, q_inv = normalize(qkv[:, :128])
    k_hat, k_inv = normalize(qkv[:, 128:256])
    q_n = q_hat.astype(BF)
    k_n = k_hat.astype(BF)
    v_n = qkv[:, 256:].astype(BF)
    expo = jnp.exp(mm_nt(q_n, k_n) * scale)
    prob = expo / jnp.sum(expo, axis=-1, keepdims=True)
    prob_n = prob.astype(BF)
    am[mine] = mm(prob_n, v_n).astype(BF)

    def gather_far(a):
        copy = copies.new(a.at[mine], a.at[mine], far)
        copy.start()
        return copy

    def gather_y(a, t):
        group = [copies.new(a.at[t], a.at[t], peer) for peer in y_peers]
        for copy in group:
            copy.start()
        return group

    m_far = gather_far(am)
    m_y = gather_y(am, mine)

    d_prob = mm_nt(d_mixed, v_n)
    d_v = mm_tn(prob_n, d_mixed)
    d_scores = prob * (d_prob - jnp.sum(prob * d_prob, axis=-1, keepdims=True)) * scale
    d_scores = d_scores.astype(BF)
    d_q = norm_back(q_hat, q_inv, mm(d_scores, k_n))
    d_k = norm_back(k_hat, k_inv, mm_tn(d_scores, q_n))
    aq[mine] = jnp.concatenate([d_q, d_k, d_v], axis=1).astype(BF)
    q_gfar = gather_far(aq)

    upper = finish(u_y, u_far, pu, lu, zu)
    erf1 = 1.0 + lax.erf(upper * (1.0 / math.sqrt(2.0)))
    ah[mine] = (0.5 * upper * erf1).astype(BF)
    h_far = gather_far(ah)
    h_y = gather_y(ah, mine)
    slope = 0.5 * erf1 + upper * jnp.exp(-0.5 * upper * upper) * (1.0 / math.sqrt(2.0 * math.pi))
    au[mine] = (sg_hidden * slope).astype(BF)
    u_gfar = gather_far(au)
    m_far.wait_recv()
    m_y2 = gather_y(am, theirs)
    q_gy = gather_y(aq, mine)
    h_far.wait_recv()
    h_y2 = gather_y(ah, theirs)
    q_gfar.wait_recv()
    q_gy2 = gather_y(aq, theirs)
    u_gy = gather_y(au, mine)
    u_gfar.wait_recv()
    u_gy2 = gather_y(au, theirs)

    cores = []
    for k in range(4):
        if k:
            wait_recv([m_y[k - 1], m_y2[k - 1], h_y[k - 1], h_y2[k - 1]])
        g = (y + 4 - k) % 4

        def out_step(i, carry, g=g):
            t = 2 * g + i
            out = mm(jnp.concatenate([ah[t], am[t]], axis=1), wb[...]).astype(BF)
            for cb in range(4):
                lp[cb % 2, cb // 2, t] = out[:, cb * 128 : cb * 128 + 128]
            return carry

        lax.fori_loop(0, 2, out_step, 0)
        copy = copies.new(lp.at[1 - c, :, pl.ds(2 * g, 2)], lc.at[:, pl.ds(2 * g, 2)], sibling)
        copy.start()
        cores.append(copy)
    wait_recv(cores)

    def core_step(t, carry):
        for b in range(2):
            s1[b, t] = (lp[c, b, t].astype(F32) + lc[b, t].astype(F32)).astype(BF)
        return carry

    lax.fori_loop(0, 8, core_step, 0)
    o_x = []
    for j, peer in enumerate(x_peers):
        copy = copies.new(s1.at[:, pl.ds(2 * ((x + j + 1) % 4), 2)], lx.at[j], peer)
        copy.start()
        o_x.append(copy)

    acc_b[...] = jnp.zeros_like(acc_b)

    def grad_b(t, carry):
        acc_b[...] += mm_tn(jnp.concatenate([ah[t], am[t]], axis=1), tokens(ga, t))
        return carry

    lax.fori_loop(0, 8, grad_b, 0)

    wait_recv(o_x)
    for b in range(2):
        for i in range(2):
            out = s1[b, 2 * x + i].astype(F32)
            for j in range(3):
                out = out + lx[j, b, i].astype(F32)
            s2[b, i] = out.astype(BF)
    o_z = []
    for j, peer in enumerate(z_peers):
        to = (zl + j + 1) % 4
        copy = copies.new(s2.at[to % 2, to // 2], lz.at[j], peer)
        copy.start()
        o_z.append(copy)

    gd_ref[...] = acc_b[0:384, :].astype(BF)
    go_ref[...] = acc_b[384:512, :].astype(BF)
    acc_x[...] = jnp.zeros_like(acc_x)

    def grad_x(g):
        def step(i, carry):
            t = 2 * g + i
            acc_x[...] += mm_tn(tokens(xa, t), jnp.concatenate([aq[t], au[t]], axis=1))
            return carry

        lax.fori_loop(0, 2, step, 0)

    grad_x(y)
    wait_recv(o_z)
    out = s2[zl % 2, zl // 2].astype(F32)
    for j in range(3):
        out = out + lz[j].astype(F32)
    s3[...] = out.astype(BF)
    o_swap = swap_start(s3, fin)
    for k in (1, 2, 3):
        wait_recv([q_gy[k - 1], q_gy2[k - 1], u_gy[k - 1], u_gy2[k - 1]])
        grad_x((y + 4 - k) % 4)
    gq_ref[...] = acc_x[:, 0:384].astype(BF)
    gu_ref[...] = acc_x[:, 384:768].astype(BF)
    o_swap()
    lay_ref[...] = (block_f + fin[...].astype(F32)).astype(BF)

    for copy in copies.all:
        copy.wait_send()

    @pl.when(moves)
    def _():
        for copy in swaps:
            copy.wait_send()


def shards(inputs, qkv_weight, out_weight, up_weight, down_weight, grad_out):
    rows = qkv_weight.shape[0]
    vmem = pl.BlockSpec(memory_space=pltpu.VMEM)

    def buf(*shape, dtype=BF):
        return pltpu.VMEM(shape, dtype)

    layer_out, qkv_grad, out_grad, up_grad, down_grad = pl.pallas_call(
        kernel,
        out_shape=[
            jax.ShapeDtypeStruct(inputs.shape, BF),
            jax.ShapeDtypeStruct((rows, 384), BF),
            jax.ShapeDtypeStruct(out_weight.shape, BF),
            jax.ShapeDtypeStruct(up_weight.shape, BF),
            jax.ShapeDtypeStruct(down_weight.shape, BF),
        ],
        in_specs=[vmem] * 6,
        out_specs=[vmem] * 5,
        scratch_shapes=[
            buf(512, 512),
            buf(TOK, 128),
            buf(2, 2, 8, TOK, 128),
            buf(2, 2, 8, TOK, 128),
            buf(10, 8, TOK, dtype=F32),
            buf(8, TOK, 512),
            buf(8, TOK, 384),
            buf(8, TOK, 384),
            buf(2, 3, TOK, 512),
            buf(2, 3, TOK, 384),
            buf(2, 3, TOK, 384),
            buf(TOK, 512),
            buf(TOK, 384),
            buf(TOK, 384),
            buf(TOK, 512),
            buf(TOK, 384),
            buf(TOK, 384),
            buf(8, TOK, 128),
            buf(8, TOK, 384),
            buf(8, TOK, 384),
            buf(8, TOK, 384),
            buf(2, 2, 8, TOK, 128),
            buf(2, 8, TOK, 128),
            buf(2, 8, TOK, 128),
            buf(3, 2, 2, TOK, 128),
            buf(2, 2, TOK, 128),
            buf(3, TOK, 128),
            buf(TOK, 128),
            buf(TOK, 128),
            buf(512, 768, dtype=F32),
            buf(512, 512, dtype=F32),
            pltpu.SemaphoreType.DMA((N_SEMS,)),
            pltpu.SemaphoreType.DMA((N_SEMS,)),
            pltpu.SemaphoreType.DMA((4,)),
        ],
        compiler_params=pltpu.CompilerParams(
            collective_id=0, has_side_effects=True, vmem_limit_bytes=56 * 2**20
        ),
    )(inputs, grad_out, qkv_weight.reshape(rows, 384), out_weight, up_weight, down_weight)
    return layer_out, qkv_grad.reshape(qkv_weight.shape), out_grad, up_grad, down_grad


def solution(mesh):
    placed = (
        P("dp", "mp"),
        P("dp", None, "mp"),
        P("mp", "dp"),
        P("dp", "mp"),
        P("mp", "dp"),
        P("dp", "mp"),
    )
    return jax.shard_map(
        shards,
        mesh=mesh,
        in_specs=placed,
        out_specs=(P("dp", "mp"), P("dp", None, "mp"), P("mp", "dp"), P("dp", "mp"), P("mp", "dp")),
        check_vma=False,
    )
```

time: 1060 us -> 191 us (0.18)
  waiting for transfers between devices: 987 us -> 0 us
  Pallas kernels: 0 us -> 182 us
  matrix products: 39.2 us -> 0 us
  between operations: 14.1 us -> 0.67 us
    reduce_scatter x5 -> x0, waiting for transfers between devices: 544 us -> none  [the longest x1 112 us: shards(): lax.psum_scatter(part_down.astype(jnp.bfloat16), 'dp', scatter_dimension=...]
    all_gather x6 -> x0, waiting for transfers between devices: 440 us -> none  [the longest x1 93.1 us: shards(): lax.all_gather(qkv_weight, 'dp', axis=0, tiled=True)]
    pallas_call x0 -> x1, Pallas kernels: none -> 182 us  [shards(): pl.pallas_call(kernel, out_shape=[jax.ShapeDtypeStruct(inputs.shape, BF),...]
    dot_general x15 -> x0, matrix products: 39.2 us -> none  [the longest x1 7.24 us: shards(): part_up = jnp.dot(normed.T, d_up, preferred_element_type=jnp.float32)]
  transfers between devices with their start and end apart: 11 -> 0, of which waited for: 11 -> 0; matrix products, arithmetic and copies ran while one was open for 5% -> 0% of each run, Pallas kernels for 0% -> 0%
where the time goes in v1:
time: 191 us
  Pallas kernels  182 us (95%)
  local copies, waits for them, and re-layouts  7.64 us (4%)
    pallas_call x1, Pallas kernels, shards(): pl.pallas_call(kernel, out_shape=[jax.ShapeDtypeStruct(inputs.shape, BF),...  182 us
    unnamed x14, local copies, waits for them, and re-layouts  5.56 us

profile of v1, /device:TPU:36, one launch (start us, length us, event | category | flops | bytes accessed | tf_op | source)
XLA Modules:
  0.0 190.6 jit_solution(13373217790324240942)
XLA Ops:
  0.6 1.2 copy.13
  1.8 0.9 copy.14.wq_ref
  2.7 182.3 %shard_map.101 = (bf16[256,128]{1,0:T(8,128)(2,1)}, bf16[512,384]{1,0:T(8,128)(2,1)}, bf16[128,512]{1,0:T(8,128)(2,1)}, bf16[512,384]{1,0:T(8,128)(2,1)}, bf16[384,512]{1,0:T(8,128)(2,1)}) custom-call(bf16[256,128]{1,0:T(8,128)(2,1)} %in_ref.1, bf16[256,128]{1,0:T(8,128)(2,1)} %grad_ref.1, bf16[512,384]{1,0:T(8,128)(2,1)} %copy.14.wq_ref, ...), custom_call_target="tpu_custom_call" | custom-call | tf_op jit(solution)/shard_map/pallas_call | solution.py:453
  185.0 1.2 copy.15
  186.2 0.0 copy-start.3
  186.2 0.0 copy-start.1
  186.2 0.9 copy.16
  187.1 0.0 copy-done.3
  187.1 0.0 copy-start.2
  187.1 0.6 copy.21
  187.8 0.3 copy-done.2
  188.1 0.7 copy.22
  188.7 0.0 copy-done.1
  188.7 0.0 copy-start
  188.7 0.7 copy.23
  189.5 0.4 copy-done
  189.9 0.7 copy.24
Async XLA Ops:
  186.2 0.9 copy-start.3
  186.2 2.5 %copy-start.1 = (bf16[512,384]{1,0:T(8,128)(2,1)S(1)}, bf16[512,384]{1,0:T(8,128)(2,1)}, u32[]{:S(2)}) copy-start(bf16[512,384]{1,0:T(8,128)(2,1)} %get-tuple-element.33) | copy-start | bytes 1179652
  187.1 0.9 copy-start.2
  188.7 1.1 copy-start

commit v2 on v1

v2 whole, which is shorter than its diff:
```python
import math

import jax
import jax.numpy as jnp
from jax import lax
from jax.experimental import pallas as pl
from jax.experimental.pallas import tpu as pltpu
from jax.sharding import PartitionSpec as P

HEAD = 128
TOK = 256
BF = jnp.bfloat16
F32 = jnp.float32
MESH = pl.DeviceIdType.MESH


def normalize(values):
    centre = values - jnp.mean(values, axis=-1, keepdims=True)
    scale_inv = 1.0 / jnp.sqrt(jnp.mean(centre * centre, axis=-1, keepdims=True) + 1e-06)
    return centre * scale_inv, scale_inv


def norm_back(normed_hat, scale_inv, upstream):
    first = jnp.mean(upstream, axis=-1, keepdims=True)
    second = jnp.mean(upstream * normed_hat, axis=-1, keepdims=True)
    return scale_inv * (upstream - first - normed_hat * second)


def mm(a, b):
    return lax.dot_general(a, b, (((1,), (0,)), ((), ())), preferred_element_type=F32)


def mm_nt(a, b):
    return lax.dot_general(a, b, (((1,), (1,)), ((), ())), preferred_element_type=F32)


def mm_tn(a, b):
    return lax.dot_general(a, b, (((0,), (0,)), ((), ())), preferred_element_type=F32)


def merge_stats(parts, count):
    means = [p[0:1, :] for p in parts]
    mean = sum(means) / len(parts)
    square = sum(p[1:2, :] for p in parts) + count * sum((u - mean) * (u - mean) for u in means)
    return mean, square


def two_rows(first, second, rows):
    place = lax.broadcasted_iota(jnp.int32, (rows, TOK), 0)
    return jnp.where(place == 0, first, jnp.where(place == 1, second, 0.0))


class Copies:
    def __init__(self, send, recv):
        self.send, self.recv, self.used, self.all = send, recv, 0, []

    def take(self, count):
        base = self.used
        self.used += count
        return base

    def make(self, src, dst, device, index):
        return pltpu.make_async_remote_copy(
            src_ref=src,
            dst_ref=dst,
            send_sem=self.send.at[index],
            recv_sem=self.recv.at[index],
            device_id=device,
            device_id_type=MESH,
        )

    def new(self, src, dst, device):
        copy = self.make(src, dst, device, self.take(1))
        self.all.append(copy)
        return copy


N_SEMS = 192


def kernel(
    in_ref, grad_ref, wq_ref, wo_ref, wu_ref, wd_ref,
    lay_ref, gq_ref, go_ref, gu_ref, gd_ref,
    wb, wq, sa, xb, ga, xa, st,
    pg, pq, pu, lg, lq, lu, rg, rq, ru, sg, sq, su, zg, zq, zu,
    am, ah, aq, au,
    lp, lc, s1, lx, s2, lz, s3, fin,
    acc_x, acc_b,
    send, recv, local,
):
    m = lax.axis_index("mp")
    d = lax.axis_index("dp")
    x, zl, c = m // 8, (m // 2) % 4, m % 2
    y, zh = d // 2, d % 2

    def at(x=x, zl=zl, c=c, y=y, zh=zh):
        return {"mp": (x * 4 + zl) * 2 + c, "dp": y * 2 + zh}

    sibling = at(c=1 - c)
    z_peers = [at(zl=(zl + j) % 4) for j in (1, 2, 3)]
    x_peers = [at(x=(x + j) % 4) for j in (1, 2, 3)]
    y_peers = [at(y=(y + k) % 4) for k in (1, 2, 3)]
    y_up, y_down = y_peers[0], y_peers[2]
    far = at(zh=1 - zh)
    swap = at(x=y, zl=2 * zh + zl % 2, y=x, zh=zl // 2)
    stays = jnp.logical_and(x == y, zh == zl // 2)
    moves = jnp.logical_not(stays)

    barrier = pltpu.get_barrier_semaphore()
    near = [sibling, far] + z_peers + x_peers + y_peers
    for device in near:
        pl.semaphore_signal(barrier, inc=1, device_id=device, device_id_type=MESH)

    @pl.when(moves)
    def _():
        pl.semaphore_signal(barrier, inc=1, device_id=swap, device_id_type=MESH)

    block_f = in_ref[...].astype(F32)
    mu = jnp.mean(block_f, axis=-1, keepdims=True)
    centre = block_f - mu
    square = jnp.sum(centre * centre, axis=-1, keepdims=True)
    lane = lax.broadcasted_iota(jnp.int32, (TOK, 128), 1)
    packed = jnp.where(lane == 0, mu, jnp.where(lane == 1, square, 0.0))
    st[0] = packed.T[0:8, :]
    wb[0:384, :] = wd_ref[...]
    wb[384:512, :] = wo_ref[...]
    for i in range(3):
        wq[:, i * 128 : i * 128 + 128] = wq_ref[i]

    @pl.when(moves)
    def _():
        pl.semaphore_wait(barrier, len(near) + 1)

    @pl.when(stays)
    def _():
        pl.semaphore_wait(barrier, len(near))

    copies = Copies(send, recv)
    swaps = []

    def swap_start(src, dst):
        remote = copies.make(src, dst, swap, copies.take(1))
        near_copy = pltpu.make_async_copy(src, dst, local.at[len(swaps)])
        swaps.append(remote)

        @pl.when(moves)
        def _():
            remote.start()

        @pl.when(stays)
        def _():
            near_copy.start()

        def wait():
            @pl.when(moves)
            def _():
                remote.wait_recv()

            @pl.when(stays)
            def _():
                near_copy.wait()

        return wait

    def send_all(block, peers):
        group = [copies.new(block, block, peer) for peer in peers]
        for copy in group:
            copy.start()
        return group

    def z_start(a):
        return send_all(a.at[c, zl % 2, x * 2 + zl // 2], z_peers)

    def half_of(a, who, half):
        return a.at[c, half, pl.ds(2 * who, 2)]

    def to_core(a, who):
        return send_all(a.at[c, :, pl.ds(2 * who, 2)], [sibling])

    def x_start(a):
        up = [copies.new(h, h, x_peers[0]) for h in (half_of(a, x, 0), half_of(a, x, 1))]
        down = [copies.new(h, h, x_peers[2]) for h in (half_of(a, x, 1), half_of(a, x, 0))]
        for pair in zip(up, down):
            for copy in pair:
                copy.start()
        return up, down

    def x_forward(a, group):
        up, down = group
        up[0].wait_recv()
        fars = send_all(half_of(a, x_before, 0), [x_peers[0]])
        down[0].wait_recv()
        fars += send_all(half_of(a, x_after, 1), [x_peers[2]])
        up[1].wait_recv()
        first = to_core(a, x_before)
        down[1].wait_recv()
        return fars, first, to_core(a, x_after)

    def wait_recv(group):
        for copy in group:
            copy.wait_recv()

    def tokens(a, t):
        return jnp.concatenate([a[0, 0, t], a[1, 0, t], a[0, 1, t], a[1, 1, t]], axis=1)

    x_before, x_after, x_far = (x + 3) % 4, (x + 1) % 4, (x + 2) % 4
    mine = d
    theirs = y * 2 + 1 - zh
    before, after = (y + 3) % 4, (y + 1) % 4
    low, high = pl.ds(0, TOK // 2), pl.ds(TOK // 2, TOK // 2)

    def group_plan(p, land, relay):
        out = []
        for own in range(2):
            to_zh = zh if own else 1 - zh
            t = [((y + k) % 4) * 2 + to_zh for k in range(4)]
            out.append([
                copies.new(p.at[t[2], low], relay.at[own, 0], y_up),
                copies.new(p.at[t[2], high], relay.at[own, 1], y_down),
                copies.new(p.at[t[1], high], land.at[own, 0, high], y_up),
                copies.new(p.at[t[3], low], land.at[own, 1, low], y_down),
            ])
        return out

    def group_send(out, who, owns):
        k = (who + 4 - y) % 4

        @pl.when(k == 2)
        def _():
            for own in owns:
                out[own][0].start()
                out[own][1].start()

        @pl.when(k == 1)
        def _():
            for own in owns:
                out[own][2].start()

        @pl.when(k == 3)
        def _():
            for own in owns:
                out[own][3].start()

    def products(p, product, who):
        def step(i, carry):
            t = 2 * who + i
            p[t] = product(t).astype(BF)
            return carry

        lax.fori_loop(0, 2, step, 0)

    def send_own(out, own):
        for copy in out[own][:4]:
            copy.start()

    def products_own(p, product, own):
        to_zh = zh if own else 1 - zh

        def step(i, carry):
            t = 2 * i + to_zh
            p[t] = product(t).astype(BF)
            return carry

        lax.fori_loop(0, 4, step, 0)

    def relay_on(out, p, land, relay, own):
        group = out[own]
        to_zh = zh if own else 1 - zh
        up, down = after * 2 + to_zh, before * 2 + to_zh
        group[0].wait_recv()
        p[up, low] = (p[up, low].astype(F32) + relay[own, 0].astype(F32)).astype(BF)
        copy = copies.new(p.at[up, low], land.at[own, 0, low], y_up)
        copy.start()
        group.append(copy)
        group[1].wait_recv()
        p[down, high] = (p[down, high].astype(F32) + relay[own, 1].astype(F32)).astype(BF)
        copy = copies.new(p.at[down, high], land.at[own, 1, high], y_down)
        copy.start()
        group.append(copy)

    def total(p, land, own, t):
        return p[t].astype(F32) + land[own, 0].astype(F32) + land[own, 1].astype(F32)

    def far_start(out, p, land, s, z):
        wait_recv(out[0][2:])
        s[...] = total(p, land, 0, theirs).astype(BF)
        copy = copies.new(s, z, far)
        copy.start()
        return copy

    def finish(out, copy, p, land, z):
        wait_recv(out[1][2:])
        copy.wait_recv()
        return total(p, land, 1, mine) + z[...].astype(F32)

    def gather_far(a):
        copy = copies.new(a.at[mine], a.at[mine], far)
        copy.start()
        return copy

    def gather_y(a, t):
        a0, a1 = a.at[t, low], a.at[t, high]
        group = [
            copies.new(a0, a0, y_up),
            copies.new(a1, a1, y_down),
            copies.new(a1, a1, y_up),
            copies.new(a0, a0, y_down),
        ]
        for copy in group:
            copy.start()
        return group

    def gather_relay(group, a, to_zh):
        group[0].wait_recv()
        block = a.at[before * 2 + to_zh, low]
        copy = copies.new(block, block, y_up)
        copy.start()
        group.append(copy)
        group[1].wait_recv()
        block = a.at[after * 2 + to_zh, high]
        copy = copies.new(block, block, y_down)
        copy.start()
        group.append(copy)

    def gather_wait(groups, k):
        for group in groups:
            if k == 1:
                group[2].wait_recv()
            elif k == 3:
                group[3].wait_recv()
            else:
                wait_recv(group[4:])

    g_swap = swap_start(grad_ref, ga.at[c, zl % 2, d])
    st_core = copies.new(st.at[0], st.at[1], sibling)
    st_core.start()
    x_swap = swap_start(in_ref, xa.at[c, zl % 2, d])
    st_core.wait_recv()
    mean, square = merge_stats([st[0], st[1]], 128.0)
    st[2] = two_rows(mean, square, 8)
    st_z = [copies.new(st.at[2], st.at[3 + j], peer) for j, peer in enumerate(z_peers)]
    for copy in st_z:
        copy.start()
    g_swap()
    g_z = z_start(ga)
    wait_recv(st_z)
    mean, square = merge_stats([st[2 + j] for j in range(4)], 256.0)
    st[6] = two_rows(mean, square, 8)
    st_x = [copies.new(st.at[6], st.at[7 + j], peer) for j, peer in enumerate(x_peers)]
    for copy in st_x:
        copy.start()
    x_swap()
    x_z = z_start(xa)
    wait_recv(g_z)
    g_x = x_start(ga)
    g_core = to_core(ga, x)
    wait_recv(st_x)
    mean, square = merge_stats([st[6 + j] for j in range(4)], 1024.0)
    inv = 1.0 / jnp.sqrt(square / 4096.0 + 1e-06)
    sa[mine] = two_rows(mean, inv, 8)
    st_far = send_all(sa.at[mine], [far])
    st_y = send_all(sa.at[mine], y_peers)
    g_out = group_plan(pg, lg, rg)
    u_out = group_plan(pu, lu, ru)
    q_out = group_plan(pq, lq, rq)

    def g_step(core, who):
        wait_recv(core)
        products(pg, lambda t: mm_nt(tokens(ga, t), wb[...]), who)
        group_send(g_out, who, (0, 1))

    def x_step(core, who):
        wait_recv(core)

        def step(i, carry):
            t = 2 * who + i
            columns = jnp.concatenate([sa[t], jnp.zeros((120, TOK), F32)], axis=0).T
            rows = tokens(xa, t).astype(F32)
            xb[t] = ((rows - columns[:, 0:1]) * columns[:, 1:2]).astype(BF)
            return carry

        lax.fori_loop(0, 2, step, 0)
        products(pu, lambda t: mm(xb[t], wu_ref[...]), who)
        group_send(u_out, who, (0,))

    g_step(g_core, x)
    g_fars, g_first, g_second = x_forward(ga, g_x)
    wait_recv(x_z)
    x_x = x_start(xa)
    x_core = to_core(xa, x)
    g_step(g_first, x_before)
    g_step(g_second, x_after)
    wait_recv(st_far)
    st_y2 = send_all(sa.at[theirs], y_peers)
    wait_recv(g_fars)
    g_step(to_core(ga, x_far), x_far)
    x_fars, x_first, x_second = x_forward(xa, x_x)
    relay_on(g_out, pg, lg, rg, 0)
    relay_on(g_out, pg, lg, rg, 1)
    wait_recv(st_y + st_y2)
    x_step(x_core, x)
    x_step(x_first, x_before)
    g_far = far_start(g_out, pg, lg, sg, zg)
    x_step(x_second, x_after)
    wait_recv(x_fars)
    x_step(to_core(xa, x_far), x_far)
    products_own(pq, lambda t: mm(xb[t], wq[...]), 0)
    send_own(q_out, 0)
    relay_on(u_out, pu, lu, ru, 0)
    send_own(u_out, 1)
    products_own(pq, lambda t: mm(xb[t], wq[...]), 1)
    relay_on(q_out, pq, lq, rq, 0)
    send_own(q_out, 1)
    u_far = far_start(u_out, pu, lu, su, zu)
    relay_on(u_out, pu, lu, ru, 1)
    q_far = far_start(q_out, pq, lq, sq, zq)
    relay_on(q_out, pq, lq, rq, 1)
    d_both = finish(g_out, g_far, pg, lg, zg)
    d_hidden = d_both[:, :384]
    d_mixed = d_both[:, 384:].astype(BF)
    upper = finish(u_out, u_far, pu, lu, zu)
    erf1 = 1.0 + lax.erf(upper * (1.0 / math.sqrt(2.0)))
    ah[mine] = (0.5 * upper * erf1).astype(BF)
    h_far = gather_far(ah)
    h_y = gather_y(ah, mine)
    slope = 0.5 * erf1 + upper * jnp.exp(-0.5 * upper * upper) * (1.0 / math.sqrt(2.0 * math.pi))
    au[mine] = (d_hidden * slope).astype(BF)
    u_gy = gather_y(au, mine)
    gather_relay(h_y, ah, zh)
    qkv = finish(q_out, q_far, pq, lq, zq)

    scale = HEAD ** (-0.5)
    q_hat, q_inv = normalize(qkv[:, :128])
    k_hat, k_inv = normalize(qkv[:, 128:256])
    q_n = q_hat.astype(BF)
    k_n = k_hat.astype(BF)
    v_n = qkv[:, 256:].astype(BF)
    expo = jnp.exp(mm_nt(q_n, k_n) * scale)
    prob = expo / jnp.sum(expo, axis=-1, keepdims=True)
    prob_n = prob.astype(BF)
    am[mine] = mm(prob_n, v_n).astype(BF)

    m_far = gather_far(am)
    m_y = gather_y(am, mine)
    u_gfar = gather_far(au)
    d_prob = mm_nt(d_mixed, v_n)
    d_v = mm_tn(prob_n, d_mixed)
    d_scores = prob * (d_prob - jnp.sum(prob * d_prob, axis=-1, keepdims=True)) * scale
    d_scores = d_scores.astype(BF)
    d_q = norm_back(q_hat, q_inv, mm(d_scores, k_n))
    d_k = norm_back(k_hat, k_inv, mm_tn(d_scores, q_n))
    aq[mine] = jnp.concatenate([d_q, d_k, d_v], axis=1).astype(BF)
    q_gfar = gather_far(aq)
    h_far.wait_recv()
    h_y2 = gather_y(ah, theirs)
    gather_relay(u_gy, au, zh)
    gather_relay(m_y, am, zh)
    m_far.wait_recv()
    m_y2 = gather_y(am, theirs)
    q_gy = gather_y(aq, mine)
    gather_relay(h_y2, ah, 1 - zh)
    gather_relay(m_y2, am, 1 - zh)
    u_gfar.wait_recv()
    u_gy2 = gather_y(au, theirs)
    gather_relay(q_gy, aq, zh)

    o_x = [
        copies.new(s1.at[:, pl.ds(2 * ((x + j) % 4), 2)], lx.at[j - 1], x_peers[j - 1])
        for j in (1, 2, 3)
    ]

    def out_product(k):
        if k:
            gather_wait([m_y, m_y2, h_y, h_y2], k)
        g = (y + 4 - k) % 4

        def out_step(i, carry, g=g):
            t = 2 * g + i
            out = mm(jnp.concatenate([ah[t], am[t]], axis=1), wb[...]).astype(BF)
            for cb in range(4):
                lp[cb % 2, cb // 2, t] = out[:, cb * 128 : cb * 128 + 128]
            return carry

        lax.fori_loop(0, 2, out_step, 0)
        copy = copies.new(lp.at[1 - c, :, pl.ds(2 * g, 2)], lc.at[:, pl.ds(2 * g, 2)], sibling)
        copy.start()
        return copy

    def out_core(copy, k):
        copy.wait_recv()
        g = (y + 4 - k) % 4

        def core_step(i, carry):
            t = 2 * g + i
            for b in range(2):
                s1[b, t] = (lp[c, b, t].astype(F32) + lc[b, t].astype(F32)).astype(BF)
            return carry

        lax.fori_loop(0, 2, core_step, 0)
        for j in (1, 2, 3):

            @pl.when((g + 4 - x) % 4 == j)
            def _():
                o_x[j - 1].start()

    c0 = out_product(0)
    c1 = out_product(1)
    c3 = out_product(3)
    out_core(c0, 0)
    c2 = out_product(2)
    out_core(c1, 1)
    out_core(c3, 3)
    out_core(c2, 2)
    gather_relay(u_gy2, au, 1 - zh)
    q_gfar.wait_recv()
    q_gy2 = gather_y(aq, theirs)
    acc_b[...] = jnp.zeros_like(acc_b)

    def grad_b(t, carry):
        acc_b[...] += mm_tn(jnp.concatenate([ah[t], am[t]], axis=1), tokens(ga, t))
        return carry

    lax.fori_loop(0, 8, grad_b, 0)

    gather_relay(q_gy2, aq, 1 - zh)
    wait_recv(o_x)
    for b in range(2):
        for i in range(2):
            out = s1[b, 2 * x + i].astype(F32)
            for j in range(3):
                out = out + lx[j, b, i].astype(F32)
            s2[b, i] = out.astype(BF)
    o_z = []
    for j, peer in enumerate(z_peers):
        to = (zl + j + 1) % 4
        copy = copies.new(s2.at[to % 2, to // 2], lz.at[j], peer)
        copy.start()
        o_z.append(copy)

    gd_ref[...] = acc_b[0:384, :].astype(BF)
    go_ref[...] = acc_b[384:512, :].astype(BF)
    acc_x[...] = jnp.zeros_like(acc_x)

    def grad_x(g):
        def step(i, carry):
            t = 2 * g + i
            acc_x[...] += mm_tn(xb[t], jnp.concatenate([aq[t], au[t]], axis=1))
            return carry

        lax.fori_loop(0, 2, step, 0)

    grad_x(y)
    wait_recv(o_z)
    out = s2[zl % 2, zl // 2].astype(F32)
    for j in range(3):
        out = out + lz[j].astype(F32)
    s3[...] = out.astype(BF)
    o_swap = swap_start(s3, fin)
    for k in (1, 3, 2):
        gather_wait([q_gy, q_gy2, u_gy, u_gy2], k)
        grad_x((y + 4 - k) % 4)
    for i in range(3):
        gq_ref[i] = acc_x[:, i * 128 : i * 128 + 128].astype(BF)
    gu_ref[...] = acc_x[:, 384:768].astype(BF)
    o_swap()
    lay_ref[...] = (block_f + fin[...].astype(F32)).astype(BF)

    for copy in copies.all:
        copy.wait_send()

    @pl.when(moves)
    def _():
        for copy in swaps:
            copy.wait_send()


def shards(inputs, qkv_weight, out_weight, up_weight, down_weight, grad_out):
    rows = qkv_weight.shape[0]
    vmem = pl.BlockSpec(memory_space=pltpu.VMEM)

    def buf(*shape, dtype=BF):
        return pltpu.VMEM(shape, dtype)

    layer_out, qkv_grad, out_grad, up_grad, down_grad = pl.pallas_call(
        kernel,
        out_shape=[
            jax.ShapeDtypeStruct(inputs.shape, BF),
            jax.ShapeDtypeStruct((3, rows, 128), BF),
            jax.ShapeDtypeStruct(out_weight.shape, BF),
            jax.ShapeDtypeStruct(up_weight.shape, BF),
            jax.ShapeDtypeStruct(down_weight.shape, BF),
        ],
        in_specs=[vmem] * 6,
        out_specs=[vmem] * 5,
        scratch_shapes=[
            buf(512, 512),
            buf(512, 384),
            buf(8, 8, TOK, dtype=F32),
            buf(8, TOK, 512),
            buf(2, 2, 8, TOK, 128),
            buf(2, 2, 8, TOK, 128),
            buf(10, 8, TOK, dtype=F32),
            buf(8, TOK, 512),
            buf(8, TOK, 384),
            buf(8, TOK, 384),
            buf(2, 2, TOK, 512),
            buf(2, 2, TOK, 384),
            buf(2, 2, TOK, 384),
            buf(2, 2, TOK // 2, 512),
            buf(2, 2, TOK // 2, 384),
            buf(2, 2, TOK // 2, 384),
            buf(TOK, 512),
            buf(TOK, 384),
            buf(TOK, 384),
            buf(TOK, 512),
            buf(TOK, 384),
            buf(TOK, 384),
            buf(8, TOK, 128),
            buf(8, TOK, 384),
            buf(8, TOK, 384),
            buf(8, TOK, 384),
            buf(2, 2, 8, TOK, 128),
            buf(2, 8, TOK, 128),
            buf(2, 8, TOK, 128),
            buf(3, 2, 2, TOK, 128),
            buf(2, 2, TOK, 128),
            buf(3, TOK, 128),
            buf(TOK, 128),
            buf(TOK, 128),
            buf(512, 768, dtype=F32),
            buf(512, 512, dtype=F32),
            pltpu.SemaphoreType.DMA((N_SEMS,)),
            pltpu.SemaphoreType.DMA((N_SEMS,)),
            pltpu.SemaphoreType.DMA((4,)),
        ],
        compiler_params=pltpu.CompilerParams(
            collective_id=0, has_side_effects=True, vmem_limit_bytes=56 * 2**20
        ),
    )(inputs, grad_out, jnp.transpose(qkv_weight, (1, 0, 2)), out_weight, up_weight, down_weight)
    return layer_out, jnp.transpose(qkv_grad, (1, 0, 2)), out_grad, up_grad, down_grad


def solution(mesh):
    placed = (
        P("dp", "mp"),
        P("dp", None, "mp"),
        P("mp", "dp"),
        P("dp", "mp"),
        P("mp", "dp"),
        P("dp", "mp"),
    )
    return jax.shard_map(
        shards,
        mesh=mesh,
        in_specs=placed,
        out_specs=(P("dp", "mp"), P("dp", None, "mp"), P("mp", "dp"), P("dp", "mp"), P("mp", "dp")),
        check_vma=False,
    )
```

time: 191 us -> 161 us (0.84)
  Pallas kernels: 182 us -> 152 us
    pallas_call x1, Pallas kernels: 182 us -> 152 us  [shards(): pl.pallas_call(kernel, out_shape=[jax.ShapeDtypeStruct(inputs.shape, BF),...]
    unnamed x14 -> x11, local copies, waits for them, and re-layouts: 5.56 us -> 5.84 us
where the time goes in v2:
time: 161 us; the launch traced here: 159 us
  Pallas kernels  152 us (94%)
  local copies, waits for them, and re-layouts  5.84 us (4%)
    pallas_call x1, Pallas kernels, shards(): pl.pallas_call(kernel, out_shape=[jax.ShapeDtypeStruct(inputs.shape, BF),...  152 us
    unnamed x11, local copies, waits for them, and re-layouts  5.84 us

profile of v2, /device:TPU:36, one launch (start us, length us, event | category | flops | bytes accessed | tf_op | source)
XLA Modules:
  0.0 158.8 jit_solution(10193461790348217572)
XLA Ops:
  0.6 152.3 %shard_map.101 = (bf16[256,128]{1,0:T(8,128)(2,1)}, bf16[3,512,128]{2,1,0:T(8,128)(2,1)}, bf16[128,512]{1,0:T(8,128)(2,1)}, bf16[512,384]{1,0:T(8,128)(2,1)}, bf16[384,512]{1,0:T(8,128)(2,1)}) custom-call(bf16[256,128]{1,0:T(8,128)(2,1)} %in_ref.1, bf16[256,128]{1,0:T(8,128)(2,1)} %grad_ref.1, bf16[3,512,128]{2,1,0:T(8,128)(2,1)} %bitcast.3, ...), custom_call_target="tpu_custom_call" | custom-call | tf_op jit(solution)/shard_map/pallas_call | solution.py:584
  152.9 1.5 copy.16
  154.4 0.0 copy-start.2
  154.4 0.0 copy-start.1
  154.4 1.8 %copy.17 = bf16[512,3,128]{2,0,1:T(8,128)(2,1)} copy(bf16[512,3,128]{2,0,1:T(8,128)(2,1)} %bitcast.2) | data formatting | bytes 786432
  156.2 0.0 copy-done.2
  156.2 0.7 copy.18
  156.9 0.0 copy-done.1
  156.9 0.0 copy-start
  156.9 0.7 copy.19
  157.6 0.4 copy-done
  158.0 0.7 copy.20
Async XLA Ops:
  154.4 1.8 %copy-start.2 = (bf16[128,512]{1,0:T(8,128)(2,1)S(1)}, bf16[128,512]{1,0:T(8,128)(2,1)}, u32[]{:S(2)}) copy-start(bf16[128,512]{1,0:T(8,128)(2,1)} %get-tuple-element.22) | copy-start | bytes 393220
  154.4 2.5 %copy-start.1 = (bf16[512,384]{1,0:T(8,128)(2,1)S(1)}, bf16[512,384]{1,0:T(8,128)(2,1)}, u32[]{:S(2)}) copy-start(bf16[512,384]{1,0:T(8,128)(2,1)} %get-tuple-element.23) | copy-start | bytes 1179652
  156.9 1.1 copy-start

commit v3 on v2

--- a/solution.py
+++ b/solution.py
@@ -331,35 +331,41 @@
             else:
                 wait_recv(group[4:])
 
-    g_swap = swap_start(grad_ref, ga.at[c, zl % 2, d])
+    x_swap = swap_start(in_ref, xa.at[c, zl % 2, d])
     st_core = copies.new(st.at[0], st.at[1], sibling)
     st_core.start()
-    x_swap = swap_start(in_ref, xa.at[c, zl % 2, d])
+    g_swap = swap_start(grad_ref, ga.at[c, zl % 2, d])
     st_core.wait_recv()
     mean, square = merge_stats([st[0], st[1]], 128.0)
     st[2] = two_rows(mean, square, 8)
     st_z = [copies.new(st.at[2], st.at[3 + j], peer) for j, peer in enumerate(z_peers)]
     for copy in st_z:
         copy.start()
-    g_swap()
-    g_z = z_start(ga)
+    x_swap()
+    x_z = z_start(xa)
     wait_recv(st_z)
     mean, square = merge_stats([st[2 + j] for j in range(4)], 256.0)
     st[6] = two_rows(mean, square, 8)
     st_x = [copies.new(st.at[6], st.at[7 + j], peer) for j, peer in enumerate(x_peers)]
     for copy in st_x:
         copy.start()
-    x_swap()
-    x_z = z_start(xa)
-    wait_recv(g_z)
-    g_x = x_start(ga)
-    g_core = to_core(ga, x)
+    g_swap()
+    g_z = z_start(ga)
+    wait_recv(x_z)
+    x_x = x_start(xa)
+    x_core = to_core(xa, x)
     wait_recv(st_x)
     mean, square = merge_stats([st[6 + j] for j in range(4)], 1024.0)
     inv = 1.0 / jnp.sqrt(square / 4096.0 + 1e-06)
     sa[mine] = two_rows(mean, inv, 8)
     st_far = send_all(sa.at[mine], [far])
     st_y = send_all(sa.at[mine], y_peers)
+    x_fars, x_first, x_second = x_forward(xa, x_x)
+    wait_recv(g_z)
+    g_x = x_start(ga)
+    g_core = to_core(ga, x)
+    wait_recv(st_far)
+    st_y2 = send_all(sa.at[theirs], y_peers)
     g_out = group_plan(pg, lg, rg)
     u_out = group_plan(pu, lu, ru)
     q_out = group_plan(pq, lq, rq)
@@ -367,7 +373,7 @@
     def g_step(core, who):
         wait_recv(core)
         products(pg, lambda t: mm_nt(tokens(ga, t), wb[...]), who)
-        group_send(g_out, who, (0, 1))
+        group_send(g_out, who, (0,))
 
     def x_step(core, who):
         wait_recv(core)
@@ -382,51 +388,36 @@
         lax.fori_loop(0, 2, step, 0)
         products(pu, lambda t: mm(xb[t], wu_ref[...]), who)
         group_send(u_out, who, (0,))
-
-    g_step(g_core, x)
-    g_fars, g_first, g_second = x_forward(ga, g_x)
-    wait_recv(x_z)
-    x_x = x_start(xa)
-    x_core = to_core(xa, x)
-    g_step(g_first, x_before)
-    g_step(g_second, x_after)
-    wait_recv(st_far)
-    st_y2 = send_all(sa.at[theirs], y_peers)
-    wait_recv(g_fars)
-    g_step(to_core(ga, x_far), x_far)
-    x_fars, x_first, x_second = x_forward(xa, x_x)
-    relay_on(g_out, pg, lg, rg, 0)
-    relay_on(g_out, pg, lg, rg, 1)
+        products(pq, lambda t: mm(xb[t], wq[...]), who)
+        group_send(q_out, who, (0,))
+
     wait_recv(st_y + st_y2)
     x_step(x_core, x)
     x_step(x_first, x_before)
-    g_far = far_start(g_out, pg, lg, sg, zg)
     x_step(x_second, x_after)
     wait_recv(x_fars)
     x_step(to_core(xa, x_far), x_far)
-    products_own(pq, lambda t: mm(xb[t], wq[...]), 0)
-    send_own(q_out, 0)
+    send_own(u_out, 1)
     relay_on(u_out, pu, lu, ru, 0)
-    send_own(u_out, 1)
-    products_own(pq, lambda t: mm(xb[t], wq[...]), 1)
+    g_fars, g_first, g_second = x_forward(ga, g_x)
     relay_on(q_out, pq, lq, rq, 0)
     send_own(q_out, 1)
     u_far = far_start(u_out, pu, lu, su, zu)
     relay_on(u_out, pu, lu, ru, 1)
     q_far = far_start(q_out, pq, lq, sq, zq)
+    g_step(g_core, x)
+    g_step(g_first, x_before)
+    g_step(g_second, x_after)
+    wait_recv(g_fars)
+    g_step(to_core(ga, x_far), x_far)
     relay_on(q_out, pq, lq, rq, 1)
-    d_both = finish(g_out, g_far, pg, lg, zg)
-    d_hidden = d_both[:, :384]
-    d_mixed = d_both[:, 384:].astype(BF)
+    send_own(g_out, 1)
     upper = finish(u_out, u_far, pu, lu, zu)
     erf1 = 1.0 + lax.erf(upper * (1.0 / math.sqrt(2.0)))
     ah[mine] = (0.5 * upper * erf1).astype(BF)
     h_far = gather_far(ah)
     h_y = gather_y(ah, mine)
     slope = 0.5 * erf1 + upper * jnp.exp(-0.5 * upper * upper) * (1.0 / math.sqrt(2.0 * math.pi))
-    au[mine] = (d_hidden * slope).astype(BF)
-    u_gy = gather_y(au, mine)
-    gather_relay(h_y, ah, zh)
     qkv = finish(q_out, q_far, pq, lq, zq)
 
     scale = HEAD ** (-0.5)
@@ -442,7 +433,22 @@
 
     m_far = gather_far(am)
     m_y = gather_y(am, mine)
+    relay_on(g_out, pg, lg, rg, 0)
+    gather_relay(h_y, ah, zh)
+    relay_on(g_out, pg, lg, rg, 1)
+    g_far = far_start(g_out, pg, lg, sg, zg)
+    h_far.wait_recv()
+    h_y2 = gather_y(ah, theirs)
+    gather_relay(m_y, am, zh)
+    m_far.wait_recv()
+    m_y2 = gather_y(am, theirs)
+    gather_relay(h_y2, ah, 1 - zh)
+    gather_relay(m_y2, am, 1 - zh)
+    d_both = finish(g_out, g_far, pg, lg, zg)
+    au[mine] = (d_both[:, :384] * slope).astype(BF)
     u_gfar = gather_far(au)
+    u_gy = gather_y(au, mine)
+    d_mixed = d_both[:, 384:].astype(BF)
     d_prob = mm_nt(d_mixed, v_n)
     d_v = mm_tn(prob_n, d_mixed)
     d_scores = prob * (d_prob - jnp.sum(prob * d_prob, axis=-1, keepdims=True)) * scale
@@ -451,18 +457,8 @@
     d_k = norm_back(k_hat, k_inv, mm_tn(d_scores, q_n))
     aq[mine] = jnp.concatenate([d_q, d_k, d_v], axis=1).astype(BF)
     q_gfar = gather_far(aq)
-    h_far.wait_recv()
-    h_y2 = gather_y(ah, theirs)
+    q_gy = gather_y(aq, mine)
     gather_relay(u_gy, au, zh)
-    gather_relay(m_y, am, zh)
-    m_far.wait_recv()
-    m_y2 = gather_y(am, theirs)
-    q_gy = gather_y(aq, mine)
-    gather_relay(h_y2, ah, 1 - zh)
-    gather_relay(m_y2, am, 1 - zh)
-    u_gfar.wait_recv()
-    u_gy2 = gather_y(au, theirs)
-    gather_relay(q_gy, aq, zh)
 
     o_x = [
         copies.new(s1.at[:, pl.ds(2 * ((x + j) % 4), 2)], lx.at[j - 1], x_peers[j - 1])
@@ -509,11 +505,14 @@
     out_core(c0, 0)
     c2 = out_product(2)
     out_core(c1, 1)
+    gather_relay(q_gy, aq, zh)
     out_core(c3, 3)
     out_core(c2, 2)
-    gather_relay(u_gy2, au, 1 - zh)
+    u_gfar.wait_recv()
+    u_gy2 = gather_y(au, theirs)
     q_gfar.wait_recv()
     q_gy2 = gather_y(aq, theirs)
+    gather_relay(u_gy2, au, 1 - zh)
     acc_b[...] = jnp.zeros_like(acc_b)
 
     def grad_b(t, carry):

time: 161 us -> 152 us (0.944); the launches traced: 159 us -> 152 us
  Pallas kernels: 152 us -> 145 us
    pallas_call x1, Pallas kernels: 152 us -> 145 us  [shards(): pl.pallas_call(kernel, out_shape=[jax.ShapeDtypeStruct(inputs.shape, BF),...]
where the time goes in v3:
time: 152 us
  Pallas kernels  145 us (95%)
  local copies, waits for them, and re-layouts  5.84 us (4%)
    pallas_call x1, Pallas kernels, shards(): pl.pallas_call(kernel, out_shape=[jax.ShapeDtypeStruct(inputs.shape, BF),...  145 us
    unnamed x11, local copies, waits for them, and re-layouts  5.84 us

profile of v3, /device:TPU:36, one launch (start us, length us, event | category | flops | bytes accessed | tf_op | source)
XLA Modules:
  0.0 151.5 jit_solution(9316553346695445244)
XLA Ops:
  0.6 145.0 %shard_map.101 = (bf16[256,128]{1,0:T(8,128)(2,1)}, bf16[3,512,128]{2,1,0:T(8,128)(2,1)}, bf16[128,512]{1,0:T(8,128)(2,1)}, bf16[512,384]{1,0:T(8,128)(2,1)}, bf16[384,512]{1,0:T(8,128)(2,1)}) custom-call(bf16[256,128]{1,0:T(8,128)(2,1)} %in_ref.1, bf16[256,128]{1,0:T(8,128)(2,1)} %grad_ref.1, bf16[3,512,128]{2,1,0:T(8,128)(2,1)} %bitcast.3, ...), custom_call_target="tpu_custom_call" | custom-call | tf_op jit(solution)/shard_map/pallas_call | solution.py:583
  145.7 1.5 copy.16
  147.2 0.0 copy-start.2
  147.2 0.0 copy-start.1
  147.2 1.8 %copy.17 = bf16[512,3,128]{2,0,1:T(8,128)(2,1)} copy(bf16[512,3,128]{2,0,1:T(8,128)(2,1)} %bitcast.2) | data formatting | bytes 786432
  149.0 0.0 copy-done.2
  149.0 0.7 copy.18
  149.7 0.0 copy-done.1
  149.7 0.0 copy-start
  149.7 0.7 copy.19
  150.4 0.4 copy-done
  150.8 0.7 copy.20
Async XLA Ops:
  147.2 1.8 %copy-start.2 = (bf16[128,512]{1,0:T(8,128)(2,1)S(1)}, bf16[128,512]{1,0:T(8,128)(2,1)}, u32[]{:S(2)}) copy-start(bf16[128,512]{1,0:T(8,128)(2,1)} %get-tuple-element.22) | copy-start | bytes 393220
  147.2 2.5 %copy-start.1 = (bf16[512,384]{1,0:T(8,128)(2,1)S(1)}, bf16[512,384]{1,0:T(8,128)(2,1)}, u32[]{:S(2)}) copy-start(bf16[512,384]{1,0:T(8,128)(2,1)} %get-tuple-element.23) | copy-start | bytes 1179652
  149.7 1.1 copy-start

commit v4 on v3

--- a/solution.py
+++ b/solution.py
@@ -334,7 +334,6 @@
     x_swap = swap_start(in_ref, xa.at[c, zl % 2, d])
     st_core = copies.new(st.at[0], st.at[1], sibling)
     st_core.start()
-    g_swap = swap_start(grad_ref, ga.at[c, zl % 2, d])
     st_core.wait_recv()
     mean, square = merge_stats([st[0], st[1]], 128.0)
     st[2] = two_rows(mean, square, 8)
@@ -343,14 +342,13 @@
         copy.start()
     x_swap()
     x_z = z_start(xa)
+    g_swap = swap_start(grad_ref, ga.at[c, zl % 2, d])
     wait_recv(st_z)
     mean, square = merge_stats([st[2 + j] for j in range(4)], 256.0)
     st[6] = two_rows(mean, square, 8)
     st_x = [copies.new(st.at[6], st.at[7 + j], peer) for j, peer in enumerate(x_peers)]
     for copy in st_x:
         copy.start()
-    g_swap()
-    g_z = z_start(ga)
     wait_recv(x_z)
     x_x = x_start(xa)
     x_core = to_core(xa, x)
@@ -361,11 +359,10 @@
     st_far = send_all(sa.at[mine], [far])
     st_y = send_all(sa.at[mine], y_peers)
     x_fars, x_first, x_second = x_forward(xa, x_x)
-    wait_recv(g_z)
-    g_x = x_start(ga)
-    g_core = to_core(ga, x)
     wait_recv(st_far)
     st_y2 = send_all(sa.at[theirs], y_peers)
+    g_swap()
+    g_z = z_start(ga)
     g_out = group_plan(pg, lg, rg)
     u_out = group_plan(pu, lu, ru)
     q_out = group_plan(pq, lq, rq)
@@ -396,7 +393,11 @@
     x_step(x_first, x_before)
     x_step(x_second, x_after)
     wait_recv(x_fars)
-    x_step(to_core(xa, x_far), x_far)
+    x_last = to_core(xa, x_far)
+    wait_recv(g_z)
+    g_x = x_start(ga)
+    g_core = to_core(ga, x)
+    x_step(x_last, x_far)
     send_own(u_out, 1)
     relay_on(u_out, pu, lu, ru, 0)
     g_fars, g_first, g_second = x_forward(ga, g_x)
@@ -458,8 +459,6 @@
     aq[mine] = jnp.concatenate([d_q, d_k, d_v], axis=1).astype(BF)
     q_gfar = gather_far(aq)
     q_gy = gather_y(aq, mine)
-    gather_relay(u_gy, au, zh)
-
     o_x = [
         copies.new(s1.at[:, pl.ds(2 * ((x + j) % 4), 2)], lx.at[j - 1], x_peers[j - 1])
         for j in (1, 2, 3)
@@ -503,10 +502,11 @@
     c1 = out_product(1)
     c3 = out_product(3)
     out_core(c0, 0)
+    gather_relay(u_gy, au, zh)
     c2 = out_product(2)
     out_core(c1, 1)
+    out_core(c3, 3)
     gather_relay(q_gy, aq, zh)
-    out_core(c3, 3)
     out_core(c2, 2)
     u_gfar.wait_recv()
     u_gy2 = gather_y(au, theirs)

time: 152 us -> 147 us (0.967)
  Pallas kernels: 145 us -> 140 us
    pallas_call x1, Pallas kernels: 145 us -> 140 us  [shards(): pl.pallas_call(kernel, out_shape=[jax.ShapeDtypeStruct(inputs.shape, BF),...]
where the time goes in v4:
time: 147 us; the launch traced here: 146 us
  Pallas kernels  140 us (95%)
  local copies, waits for them, and re-layouts  5.84 us (4%)
    pallas_call x1, Pallas kernels, shards(): pl.pallas_call(kernel, out_shape=[jax.ShapeDtypeStruct(inputs.shape, BF),...  140 us
    unnamed x11, local copies, waits for them, and re-layouts  5.84 us

profile of v4, /device:TPU:36, one launch (start us, length us, event | category | flops | bytes accessed | tf_op | source)
XLA Modules:
  0.0 146.2 jit_solution(9353852942598379248)
XLA Ops:
  0.6 139.7 %shard_map.101 = (bf16[256,128]{1,0:T(8,128)(2,1)}, bf16[3,512,128]{2,1,0:T(8,128)(2,1)}, bf16[128,512]{1,0:T(8,128)(2,1)}, bf16[512,384]{1,0:T(8,128)(2,1)}, bf16[384,512]{1,0:T(8,128)(2,1)}) custom-call(bf16[256,128]{1,0:T(8,128)(2,1)} %in_ref.1, bf16[256,128]{1,0:T(8,128)(2,1)} %grad_ref.1, bf16[3,512,128]{2,1,0:T(8,128)(2,1)} %bitcast.3, ...), custom_call_target="tpu_custom_call" | custom-call | tf_op jit(solution)/shard_map/pallas_call | solution.py:583
  140.4 1.5 %copy.16 = bf16[256,128]{1,0:T(8,128)(2,1)} copy(bf16[256,128]{1,0:T(8,128)(2,1)} %get-tuple-element.20) | data formatting | bytes 131072
  141.8 0.0 copy-start.2
  141.8 0.0 copy-start.1
  141.8 1.8 %copy.17 = bf16[512,3,128]{2,0,1:T(8,128)(2,1)} copy(bf16[512,3,128]{2,0,1:T(8,128)(2,1)} %bitcast.2) | data formatting | bytes 786432
  143.7 0.0 copy-done.2
  143.7 0.7 copy.18
  144.3 0.0 copy-done.1
  144.3 0.0 copy-start
  144.3 0.7 copy.19
  145.1 0.4 copy-done
  145.5 0.7 copy.20
Async XLA Ops:
  141.8 1.8 %copy-start.2 = (bf16[128,512]{1,0:T(8,128)(2,1)S(1)}, bf16[128,512]{1,0:T(8,128)(2,1)}, u32[]{:S(2)}) copy-start(bf16[128,512]{1,0:T(8,128)(2,1)} %get-tuple-element.22) | copy-start | bytes 393220
  141.8 2.5 %copy-start.1 = (bf16[512,384]{1,0:T(8,128)(2,1)S(1)}, bf16[512,384]{1,0:T(8,128)(2,1)}, u32[]{:S(2)}) copy-start(bf16[512,384]{1,0:T(8,128)(2,1)} %get-tuple-element.23) | copy-start | bytes 1179652
  144.3 1.1 copy-start

commit v5 on v4

--- a/solution.py
+++ b/solution.py
@@ -507,9 +507,9 @@
     out_core(c1, 1)
     out_core(c3, 3)
     gather_relay(q_gy, aq, zh)
-    out_core(c2, 2)
     u_gfar.wait_recv()
     u_gy2 = gather_y(au, theirs)
+    out_core(c2, 2)
     q_gfar.wait_recv()
     q_gy2 = gather_y(aq, theirs)
     gather_relay(u_gy2, au, 1 - zh)

time: 147 us -> 151 us (1.027)
  Pallas kernels: 140 us -> 143 us
    pallas_call x1, Pallas kernels: 140 us -> 143 us  [shards(): pl.pallas_call(kernel, out_shape=[jax.ShapeDtypeStruct(inputs.shape, BF),...]
where the time goes in v5:
time: 151 us; the launch traced here: 149 us
  Pallas kernels  143 us (95%)
  local copies, waits for them, and re-layouts  5.84 us (4%)
    pallas_call x1, Pallas kernels, shards(): pl.pallas_call(kernel, out_shape=[jax.ShapeDtypeStruct(inputs.shape, BF),...  143 us
    unnamed x11, local copies, waits for them, and re-layouts  5.84 us

profile of v5, /device:TPU:36, one launch (start us, length us, event | category | flops | bytes accessed | tf_op | source)
XLA Modules:
  0.0 149.3 jit_solution(1117981155358962718)
XLA Ops:
  0.6 142.8 %shard_map.101 = (bf16[256,128]{1,0:T(8,128)(2,1)}, bf16[3,512,128]{2,1,0:T(8,128)(2,1)}, bf16[128,512]{1,0:T(8,128)(2,1)}, bf16[512,384]{1,0:T(8,128)(2,1)}, bf16[384,512]{1,0:T(8,128)(2,1)}) custom-call(bf16[256,128]{1,0:T(8,128)(2,1)} %in_ref.1, bf16[256,128]{1,0:T(8,128)(2,1)} %grad_ref.1, bf16[3,512,128]{2,1,0:T(8,128)(2,1)} %bitcast.3, ...), custom_call_target="tpu_custom_call" | custom-call | tf_op jit(solution)/shard_map/pallas_call | solution.py:583
  143.5 1.5 copy.16
  145.0 0.0 copy-start.2
  145.0 0.0 copy-start.1
  145.0 1.8 %copy.17 = bf16[512,3,128]{2,0,1:T(8,128)(2,1)} copy(bf16[512,3,128]{2,0,1:T(8,128)(2,1)} %bitcast.2) | data formatting | bytes 786432
  146.8 0.0 copy-done.2
  146.8 0.7 copy.18
  147.5 0.0 copy-done.1
  147.5 0.0 copy-start
  147.5 0.7 copy.19
  148.2 0.4 copy-done
  148.6 0.7 copy.20
Async XLA Ops:
  145.0 1.8 %copy-start.2 = (bf16[128,512]{1,0:T(8,128)(2,1)S(1)}, bf16[128,512]{1,0:T(8,128)(2,1)}, u32[]{:S(2)}) copy-start(bf16[128,512]{1,0:T(8,128)(2,1)} %get-tuple-element.22) | copy-start | bytes 393220
  145.0 2.5 %copy-start.1 = (bf16[512,384]{1,0:T(8,128)(2,1)S(1)}, bf16[512,384]{1,0:T(8,128)(2,1)}, u32[]{:S(2)}) copy-start(bf16[512,384]{1,0:T(8,128)(2,1)} %get-tuple-element.23) | copy-start | bytes 1179652
  147.5 1.1 copy-start
